TPU v7x, 32 devices: a whole 2x2x4 slice. The times are simulated.
32 devices in a mesh: feat: 8 (over z, x), blk: 4 (over y, core).
Axes of the slice: x: 2, y: 2, z: 4, core: 2. Of those that a mesh axis runs over, the one named last changes fastest.
Arguments:
- features: bfloat16 [1024, 8, 4096], P('feat', None, 'blk'), may hold values from -6 to 6
- adj_local: bfloat16 [32768, 1024], P(('feat', 'blk')), may hold values from 0.049804688 to 1
- adj_remote: bfloat16 [32768, 768], P(('feat', 'blk')), may hold values from 0.049804688 to 1
- tile_mask: int32 [256, 14], P(('feat', 'blk')), may hold values from 0 to 1, as said below
- w_self: bfloat16 [1024, 256], replicated, may hold values from -0.1875 to 0.1875
- w_neigh: bfloat16 [1024, 256], replicated, may hold values from -0.1875 to 0.1875
- out_bias: float32 [256], replicated, may hold values from -4 to 4
Outputs:
- hidden_out: bfloat16 [32768, 256], P(('feat', 'blk'))
Inputs may be any that keep to these rules, and one draw needn't show every extreme that they name: `tile_mask`: 0 or 1 for each tile; the 128 x 128 tiles on the diagonal of every node's adj_local block are 1.
All inputs are finite; a program needn't handle non-finite values.
Results may differ from a plain program's by a relative error of at most 0.0035.
Values may be sent and summed in bfloat16 or wider, within the bound.
A program may use at most 128 MiB of HBM per device.

v0:
```python
import jax
import jax.numpy as jnp
from jax import lax
from jax.sharding import PartitionSpec as P

TILE = 128


def passed_along(x, axis, by):
    peers = lax.axis_size(axis)
    return lax.ppermute(x, axis, [(i, (i + by) % peers) for i in range(peers)])


def expand_tiles(adjacency, tile_flags):
    row_total, col_total = adjacency.shape
    blocked = adjacency.reshape(row_total // TILE, TILE, col_total // TILE, TILE)
    blocked = blocked * tile_flags.astype(jnp.bfloat16)[:, None, :, None]
    return blocked.reshape(row_total, col_total)


def split_product(weight_piece, dense_panel):
    upper_part = dense_panel.astype(jnp.bfloat16)
    lower_part = (dense_panel - upper_part.astype(jnp.float32)).astype(jnp.bfloat16)
    first_term = jnp.dot(weight_piece, upper_part, preferred_element_type=jnp.float32)
    return first_term + jnp.dot(weight_piece, lower_part, preferred_element_type=jnp.float32)


def shards(features, adj_local, adj_remote, tile_mask, w_self, w_neigh, out_bias):
    cycle_size = lax.axis_size("blk")
    node_count = adj_local.shape[0]
    halo_len = adj_remote.shape[1] // (cycle_size - 1)
    local_tiles = node_count // TILE
    live_local = expand_tiles(adj_local, tile_mask[:, :local_tiles])
    live_remote = expand_tiles(adj_remote, tile_mask[:, local_tiles:])
    degree = jnp.sum(live_local, axis=1, dtype=jnp.float32) + jnp.sum(
        live_remote, axis=1, dtype=jnp.float32
    )
    contract_first = (((0,), (0,)), ((), ()))
    regrouped = lax.all_to_all(features, "feat", split_axis=1, concat_axis=0, tiled=True)
    own_feats = regrouped.reshape(regrouped.shape[0], node_count)
    self_term = lax.dot_general(
        own_feats, w_self, contract_first, preferred_element_type=jnp.float32
    )
    projected = lax.dot_general(
        own_feats, w_neigh, contract_first, preferred_element_type=jnp.float32
    )
    summed = split_product(live_local, projected)
    halo_panel = projected[:halo_len]
    for offset in range(1, cycle_size):
        halo_panel = passed_along(halo_panel.astype(jnp.bfloat16), "blk", 1).astype(
            halo_panel.dtype
        )
        weight_piece = live_remote[:, (offset - 1) * halo_len : offset * halo_len]
        summed = summed + split_product(weight_piece, halo_panel)
    neigh_term = summed / jnp.sqrt(degree)[:, None]
    return jax.nn.relu(self_term + neigh_term + out_bias[None, :]).astype(jnp.bfloat16)


def solution(mesh):
    placed = (
        P("feat", None, "blk"),
        P(("feat", "blk"), None),
        P(("feat", "blk"), None),
        P(("feat", "blk"), None),
        P(),
        P(),
        P(),
    )
    return jax.shard_map(
        shards, mesh=mesh, in_specs=placed, out_specs=P(("feat", "blk"), None), check_vma=False
    )
```

profile of v0, /device:TPU:0, one launch (start us, length us, event | category | flops | bytes accessed | tf_op | source)
XLA Modules:
  0.0 78.4 jit_solution(4713329572125607051)
XLA Ops:
  0.0 0.0 copy-start
  0.0 4.1 %copy.8 = bf16[128,8,1024]{2,0,1:T(8,128)(2,1)} copy(bf16[128,8,1024]{2,1,0:T(8,128)(2,1)} %param.7) | data formatting | bytes 4194304 | tf_op args[0]
  4.1 7.4 %all-to-all-start = ((bf16[128,8,1024]{2,0,1:T(8,128)(2,1)}), bf16[128,8,1024]{2,0,1:T(8,128)(2,1)}, u32[]{:S(2)}, u32[]{:S(2)}) async-start(bf16[128,8,1024]{2,0,1:T(8,128)(2,1)} %copy.8), calls=%async_computation | async-start | bytes 4194304 | tf_op jit(solution)/shard_map/all_to_all | solution.py:39
  11.5 1.7 %copy.10 = bf16[1024,768]{0,1:T(8,128)(2,1)S(1)} copy(bf16[1024,768]{1,0:T(8,128)(2,1)} %param.9) | data formatting | bytes 3145728 | tf_op args[2]
  13.2 0.1 slice.22
  13.3 0.1 copy.9
  13.4 0.3 mul.25
  13.7 1.9 %convert_reduce_fusion.1 = (f32[1024]{0:T(1024)S(1)}, bf16[1024,768]{0,1:T(8,128)(2,1)}) fusion(bf16[1024,768]{0,1:T(8,128)(2,1)S(1)} %copy.10, bf16[96,8,8,128]{3,2,1,0:T(8,128)(2,1)S(1)} %bitcast.32), kind=kLoop, calls=%fused_computation.1 | loop fusion | flops 2358272 | bytes 4722688 | tf_op jit(solution)/shard_map/reduce_sum | solution.py:35
  15.6 0.3 mul.22
  16.0 1.2 %copy-done.2 = bf16[1024,1024]{1,0:T(8,128)(2,1)S(1)} copy-done((bf16[1024,1024]{1,0:T(8,128)(2,1)S(1)}, bf16[1024,1024]{1,0:T(8,128)(2,1)}, u32[]{:S(2)}) %copy-start.2) | copy-done | bytes 2097176
  17.2 0.6 convert_reduce_fusion
  17.8 42.0 %all-to-all-done = bf16[128,8,1024]{2,0,1:T(8,128)(2,1)} async-done(((bf16[128,8,1024]{2,0,1:T(8,128)(2,1)}), bf16[128,8,1024]{2,0,1:T(8,128)(2,1)}, u32[]{:S(2)}, u32[]{:S(2)}) %all-to-all-start) | async-done | bytes 2097184 | tf_op jit(solution)/shard_map/all_to_all | solution.py:39
  59.8 2.5 %fusion.18 = (bf16[1024,256]{1,0:T(8,128)(2,1)S(1)}, f32[1024,256]{1,0:T(8,128)S(1)}) fusion(bf16[1024,1024]{1,0:T(8,128)(2,1)} %bitcast.2, bf16[1024,256]{1,0:T(8,128)(2,1)S(1)} %copy-done), kind=kOutput, calls=%fused_computation.31 | convolution fusion | flops 537133056 | bytes 4194304 | tf_op jit(solution)/shard_map/dot_general | solution.py:44
  62.3 0.7 fusion.17
  63.1 0.1 collective-permute-start
  63.1 0.0 copy-start.5
  63.2 0.7 convolution_add_fusion.3
  63.9 0.3 copy-done.5
  64.2 2.5 %fusion.19 = f32[1024,256]{1,0:T(8,128)S(1)} fusion(bf16[1024,1024]{1,0:T(8,128)(2,1)} %bitcast.2, bf16[1024,256]{1,0:T(8,128)(2,1)S(1)} %copy-done.5), kind=kOutput, calls=%fused_computation.32 | convolution fusion | flops 536870912 | bytes 3670016 | tf_op jit(solution)/shard_map/dot_general | solution.py:41
  66.7 0.9 %collective-permute-done = bf16[256,256]{1,0:T(8,128)(2,1)S(1)} collective-permute-done((bf16[256,256]{1,0:T(8,128)(2,1)S(1)}, bf16[256,256]{1,0:T(8,128)(2,1)S(1)}, u32[]{:S(2)}, u32[]{:S(2)}) %collective-permute-start) | collective-permute-done | bytes 131104 | tf_op jit(solution)/shard_map/ppermute | solution.py:11
  67.5 0.8 %collective-permute-start.1 = (bf16[256,256]{1,0:T(8,128)(2,1)S(1)}, bf16[256,256]{1,0:T(8,128)(2,1)S(1)}, u32[]{:S(2)}, u32[]{:S(2)}) collective-permute-start(bf16[256,256]{1,0:T(8,128)(2,1)S(1)} %collective-permute-done), channel_id=1, source_target_pairs={{0,1},{1,2},{2,3},{3,0},{4,5},{5,6},{6,7},{7,4},{8,9},{9,10},{10,1... | collective-permute-start | bytes 393224 | tf_op jit(solution)/shard_map/ppermute | solution.py:11
  68.3 0.0 copy-done.1
  68.3 0.4 fusion.14
  68.7 0.4 fusion.6
  69.1 2.8 %collective-permute-done.1 = bf16[256,256]{1,0:T(8,128)(2,1)S(1)} collective-permute-done((bf16[256,256]{1,0:T(8,128)(2,1)S(1)}, bf16[256,256]{1,0:T(8,128)(2,1)S(1)}, u32[]{:S(2)}, u32[]{:S(2)}) %collective-permute-start.1) | collective-permute-done | bytes 131104 | tf_op jit(solution)/shard_map/ppermute | solution.py:11
  71.9 0.3 fusion.11
  72.3 0.0 copy-start.6
  72.3 0.1 collective-permute-start.2
  72.3 0.3 fusion.5
  72.7 4.0 %collective-permute-done.2 = bf16[256,256]{1,0:T(8,128)(2,1)S(1)} collective-permute-done((bf16[256,256]{1,0:T(8,128)(2,1)S(1)}, bf16[256,256]{1,0:T(8,128)(2,1)S(1)}, u32[]{:S(2)}, u32[]{:S(2)}) %collective-permute-start.2) | collective-permute-done | bytes 131104 | tf_op jit(solution)/shard_map/ppermute | solution.py:11
  76.7 0.4 fusion.8
  77.1 1.3 %fusion.7 = bf16[1024,256]{1,0:T(8,128)(2,1)} fusion(f32[1024,256]{1,0:T(8,128)S(1)} %fusion.19, f32[1024,256]{1,0:T(8,128)S(1)} %fusion.5, f32[1024,256]{1,0:T(8,128)S(1)} %fusion.8, bf16[256,256]{1,0:T(8,128)(2,1)S(1)} %collective-permute-done.2, f32[256]{0:T(256)S(1)} %copy-done.6, f32[1024]{0:T(1024)S(1)} %add_sqrt_fusion, ...), kind=kOutput, calls=%fused_computation.15 | convolution fusion | flops 136052736 | bytes 4330496 | tf_op jit(solution)/shard_map/dot_general | solution.py:24
  (11 shorter events, 0.0 us)
Async XLA Ops:
  0.0 59.8 %copy-start = (bf16[1024,256]{1,0:T(8,128)(2,1)S(1)}, bf16[1024,256]{1,0:T(8,128)(2,1)}, u32[]{:S(2)}) copy-start(bf16[1024,256]{1,0:T(8,128)(2,1)} %param.12) | copy-start | bytes 1572868
  4.1 7.4 %copy-start.4 = (s32[8,14]{1,0:T(8,128)S(1)}, s32[8,14]{1,0:T(8,128)}, u32[]{:S(2)}) copy-start(s32[8,14]{1,0:T(8,128)} %param.10) | copy-start | bytes 1348
  4.1 55.7 %all-to-all-start = ((bf16[128,8,1024]{2,0,1:T(8,128)(2,1)}), bf16[128,8,1024]{2,0,1:T(8,128)(2,1)}, u32[]{:S(2)}, u32[]{:S(2)}) async-start(bf16[128,8,1024]{2,0,1:T(8,128)(2,1)} %copy.8), calls=%async_computation | async-start | bytes 4194304 | tf_op jit(solution)/shard_map/all_to_all | solution.py:39
  15.6 1.6 %copy-start.2 = (bf16[1024,1024]{1,0:T(8,128)(2,1)S(1)}, bf16[1024,1024]{1,0:T(8,128)(2,1)}, u32[]{:S(2)}) copy-start(bf16[1024,1024]{1,0:T(8,128)(2,1)} %param.8) | copy-start | bytes 6291460
  59.8 2.5 %copy-start.3 = (bf16[1024,1024]{1,0:T(8,128)(2,1)S(1)}, bf16[1024,1024]{1,0:T(8,128)(2,1)}, u32[]{:S(2)}) copy-start(bf16[1024,1024]{1,0:T(8,128)(2,1)} %param.8) | copy-start | bytes 6291460
  63.1 4.4 %collective-permute-start = (bf16[256,256]{1,0:T(8,128)(2,1)S(1)}, bf16[256,256]{1,0:T(8,128)(2,1)S(1)}, u32[]{:S(2)}, u32[]{:S(2)}) collective-permute-start(bf16[256,256]{1,0:T(8,128)(2,1)S(1)} %slice.28), channel_id=1, source_target_pairs={{0,1},{1,2},{2,3},{3,0},{4,5},{5,6},{6,7},{7,4},{8,9},{9,10},{10,1... | collective-permute-start | bytes 393224 | tf_op jit(solution)/shard_map/ppermute | solution.py:11
  63.1 1.0 %copy-start.5 = (bf16[1024,256]{1,0:T(8,128)(2,1)S(1)}, bf16[1024,256]{1,0:T(8,128)(2,1)}, u32[]{:S(2)}) copy-start(bf16[1024,256]{1,0:T(8,128)(2,1)} %param.11) | copy-start | bytes 1572868
  64.2 4.2 %copy-start.1 = (bf16[1024,768]{0,1:T(8,128)(2,1)S(1)}, bf16[1024,768]{0,1:T(8,128)(2,1)}, u32[]{:S(2)}) copy-start(bf16[1024,768]{0,1:T(8,128)(2,1)} %get-tuple-element.6) | copy-start | bytes 4718596
  67.5 4.4 %collective-permute-start.1 = (bf16[256,256]{1,0:T(8,128)(2,1)S(1)}, bf16[256,256]{1,0:T(8,128)(2,1)S(1)}, u32[]{:S(2)}, u32[]{:S(2)}) collective-permute-start(bf16[256,256]{1,0:T(8,128)(2,1)S(1)} %collective-permute-done), channel_id=1, source_target_pairs={{0,1},{1,2},{2,3},{3,0},{4,5},{5,6},{6,7},{7,4},{8,9},{9,10},{10,1... | collective-permute-start | bytes 393224 | tf_op jit(solution)/shard_map/ppermute | solution.py:11
  72.3 4.8 %copy-start.6 = (f32[256]{0:T(256)S(1)}, f32[256]{0:T(256)}, u32[]{:S(2)}) copy-start(f32[256]{0:T(256)} %param.13) | copy-start | bytes 3076
  72.3 4.4 %collective-permute-start.2 = (bf16[256,256]{1,0:T(8,128)(2,1)S(1)}, bf16[256,256]{1,0:T(8,128)(2,1)S(1)}, u32[]{:S(2)}, u32[]{:S(2)}) collective-permute-start(bf16[256,256]{1,0:T(8,128)(2,1)S(1)} %collective-permute-done.1), channel_id=1, source_target_pairs={{0,1},{1,2},{2,3},{3,0},{4,5},{5,6},{6,7},{7,4},{8,9},{9,10},{10,1... | collective-permute-start | bytes 393224 | tf_op jit(solution)/shard_map/ppermute | solution.py:11
where the time goes:
time: 78.7 us; the launch traced here: 78.4 us
  waiting for transfers between devices  49.7 us (63%)
  matrix products  9.49 us (12%)
  starting transfers between devices  8.32 us (11%)
  local copies, waits for them, and re-layouts  8.18 us (10%)
  other arithmetic  2.55 us (3%)
    all_to_all x1, waiting for transfers between devices, shards(): lax.all_to_all(features, 'feat', split_axis=1, concat_axis=0, tiled=True)  42 us
    ppermute x3, waiting for transfers between devices, passed_along(): return lax.ppermute(x, axis, [(i, (i + by) % peers) for i in range(peers)])  7.71 us
    unnamed x16, local copies, waits for them, and re-layouts  7.39 us
    all_to_all x1, starting transfers between devices, shards(): lax.all_to_all(features, 'feat', split_axis=1, concat_axis=0, tiled=True)  7.38 us
    dot_general x4, matrix products, split_product(): jnp.dot(weight_piece, upper_part, preferred_element_type=jnp.float32)  2.77 us
    dot_general x1, matrix products, shards(): lax.dot_general(own_feats, w_neigh, contract_first, preferred_element_typ...  2.48 us
    dot_general x1, matrix products, shards(): lax.dot_general(own_feats, w_self, contract_first, preferred_element_type...  2.46 us
    reduce_sum x1, other arithmetic, shards(): jnp.sum(live_remote, axis=1, dtype=jnp.float32)  1.92 us
  transfers between devices with their start and end apart: 4, of which 4 were waited for; matrix products, arithmetic and copies ran while one was open for 12% of the time, Pallas kernels for 0%

commit v1 on v0

v1 whole, which is shorter than its diff:
```python
import functools

import jax
import jax.numpy as jnp
from jax import lax
from jax.experimental import pallas as pl
from jax.experimental.pallas import tpu as pltpu
from jax.sharding import PartitionSpec as P

TILE = 128
CHUNK = 128
MESH = pl.DeviceIdType.MESH


def far_first(count):
    return sorted(range(1, count), key=lambda d: abs(2 * d - count))


def layer_kernel(
    parts, blocks,
    features, adj_local, adj_remote, tile_mask, w_self, w_neigh, out_bias, out,
    loaded, spread, outgoing, own, live, mask, weights, bias,
    projected, halo, self_bias, total, inverse,
    load_sem, misc_sem, send_sem, recv_sem, halo_send, halo_recv,
):
    width = features.shape[0]
    nodes = features.shape[2]
    hidden = w_self.shape[1]
    remote = adj_remote.shape[1]
    halo_len = remote // (blocks - 1)
    chunks = nodes // CHUNK
    halo_chunks = halo_len // CHUNK
    row_tiles = nodes // TILE
    local_tiles = nodes // TILE
    col_tiles = local_tiles + remote // TILE
    me = lax.axis_index("feat")
    my_block = lax.axis_index("blk")
    peers = [lax.rem(me + d, parts) for d in far_first(parts)]
    block_peers = [lax.rem(my_block + k, blocks) for k in range(1, blocks)]

    barrier = pltpu.get_barrier_semaphore()
    for peer in peers:
        pl.semaphore_signal(barrier, inc=1, device_id={"feat": peer}, device_id_type=MESH)
    for peer in block_peers:
        pl.semaphore_signal(barrier, inc=1, device_id={"blk": peer}, device_id_type=MESH)

    def load(k):
        columns = pl.ds(pl.multiple_of(k * CHUNK, CHUNK), CHUNK)
        return pltpu.make_async_copy(features.at[:, :, columns], loaded.at[k], load_sem.at[k])

    others = [
        pltpu.make_async_copy(tile_mask, mask, misc_sem.at[0]),
        pltpu.make_async_copy(out_bias, bias, misc_sem.at[1]),
        pltpu.make_async_copy(w_self, weights.at[:, pl.ds(0, hidden)], misc_sem.at[2]),
        pltpu.make_async_copy(w_neigh, weights.at[:, pl.ds(hidden, hidden)], misc_sem.at[3]),
        pltpu.make_async_copy(adj_local, live.at[:, pl.ds(0, nodes)], misc_sem.at[4]),
        pltpu.make_async_copy(adj_remote, live.at[:, pl.ds(nodes, remote)], misc_sem.at[5]),
    ]
    for k in range(chunks):
        load(k).start()
    for copy in others:
        copy.start()

    def rows_of(part):
        return pl.ds(pl.multiple_of(part * width, width), width)

    def send(k, peer):
        return pltpu.make_async_remote_copy(
            src_ref=outgoing.at[k, peer],
            dst_ref=own.at[k, rows_of(me)],
            send_sem=send_sem.at[k, peer],
            recv_sem=recv_sem.at[k, me],
            device_id={"feat": peer},
            device_id_type=MESH,
        )

    def arrival(k, peer):
        return pltpu.make_async_remote_copy(
            src_ref=outgoing.at[k, peer],
            dst_ref=own.at[k, rows_of(peer)],
            send_sem=send_sem.at[k, peer],
            recv_sem=recv_sem.at[k, peer],
            device_id={"feat": peer},
            device_id_type=MESH,
        )

    def regroup(k):
        load(k).wait()
        spread[...] = loaded[k].astype(jnp.float32).reshape(width * parts, CHUNK)
        for g in range(parts):
            outgoing[k, g] = spread[pl.ds(g, width, stride=parts), :].astype(jnp.bfloat16)

    def dispatch(k):
        for peer in peers:
            send(k, peer).start()
        own[k, rows_of(me)] = outgoing[k, me]

    regroup(0)
    pl.semaphore_wait(barrier, parts - 1 + blocks - 1)
    dispatch(0)

    @pl.loop(1, chunks)
    def _(k):
        regroup(k)
        dispatch(k)

    for copy in others:
        copy.wait()

    @pl.loop(0, row_tiles)
    def _(i):
        rows = pl.ds(pl.multiple_of(i * TILE, TILE), TILE)
        sums = jnp.zeros((TILE, TILE), jnp.float32)
        for j in range(col_tiles):
            columns = pl.ds(j * TILE, TILE)
            piece = live[rows, columns].astype(jnp.float32) * mask[i, j].astype(jnp.float32)
            live[rows, columns] = piece.astype(jnp.bfloat16)
            sums = sums + piece
        degree = jnp.sum(sums, axis=1, keepdims=True)
        inverse[rows, :] = jnp.broadcast_to(1.0 / jnp.sqrt(degree), (TILE, TILE))
        total[rows, :] = jnp.zeros((TILE, hidden), jnp.float32)

    bias_row = bias[...].reshape(1, hidden)

    def project(k):
        for peer in peers:
            arrival(k, peer).wait_recv()
        both = lax.dot_general(
            own[k], weights[...], (((0,), (0,)), ((), ())), preferred_element_type=jnp.float32
        )
        rows = pl.ds(pl.multiple_of(k * CHUNK, CHUNK), CHUNK)
        self_bias[rows, :] = both[:, :hidden] + bias_row
        projected[rows, :] = both[:, hidden:].astype(jnp.bfloat16)

    def add_local(k):
        span = pl.ds(pl.multiple_of(k * CHUNK, CHUNK), CHUNK)
        panel = projected[span, :]

        @pl.loop(0, row_tiles)
        def _(i):
            rows = pl.ds(pl.multiple_of(i * TILE, TILE), TILE)
            total[rows, :] += jnp.dot(live[rows, span], panel, preferred_element_type=jnp.float32)

    def halo_copy(slot, peer):
        return pltpu.make_async_remote_copy(
            src_ref=projected.at[pl.ds(0, halo_len)],
            dst_ref=halo.at[pl.ds(slot * halo_len, halo_len)],
            send_sem=halo_send.at[slot],
            recv_sem=halo_recv.at[slot],
            device_id={"blk": peer},
            device_id_type=MESH,
        )

    @pl.loop(0, halo_chunks)
    def _(k):
        project(k)

    for slot, peer in enumerate(block_peers):
        halo_copy(slot, peer).start()

    @pl.loop(0, halo_chunks)
    def _(k):
        add_local(k)

    for slot, peer in enumerate(block_peers):
        halo_copy(slot, peer).wait()

    @pl.loop(0, row_tiles)
    def _(i):
        rows = pl.ds(pl.multiple_of(i * TILE, TILE), TILE)
        total[rows, :] += jnp.dot(
            live[rows, pl.ds(nodes, remote)], halo[...], preferred_element_type=jnp.float32
        )

    @pl.loop(halo_chunks, chunks - 1)
    def _(k):
        project(k)
        add_local(k)

    last = chunks - 1
    project(last)
    span = pl.ds(last * CHUNK, CHUNK)
    panel = projected[span, :]

    @pl.loop(0, row_tiles)
    def _(i):
        rows = pl.ds(pl.multiple_of(i * TILE, TILE), TILE)
        summed = total[rows, :] + jnp.dot(
            live[rows, span], panel, preferred_element_type=jnp.float32
        )
        scale = jnp.concatenate([inverse[rows, :]] * (hidden // TILE), axis=1)
        out[rows, :] = jnp.maximum(self_bias[rows, :] + summed * scale, 0.0).astype(jnp.bfloat16)

    @pl.loop(0, chunks)
    def _(k):
        for peer in peers:
            arrival(k, peer).wait_send()


def shards(features, adj_local, adj_remote, tile_mask, w_self, w_neigh, out_bias):
    parts = lax.axis_size("feat")
    blocks = lax.axis_size("blk")
    width, _, nodes = features.shape
    hidden = w_self.shape[1]
    remote = adj_remote.shape[1]
    chunks = nodes // CHUNK
    bf16, f32 = jnp.bfloat16, jnp.float32
    hbm = pl.BlockSpec(memory_space=pltpu.HBM)
    return pl.pallas_call(
        functools.partial(layer_kernel, parts, blocks),
        out_shape=jax.ShapeDtypeStruct((nodes, hidden), bf16),
        in_specs=[hbm] * 7,
        out_specs=pl.BlockSpec(memory_space=pltpu.VMEM),
        scratch_shapes=[
            pltpu.VMEM((chunks, width, parts, CHUNK), bf16),
            pltpu.VMEM((width * parts, CHUNK), f32),
            pltpu.VMEM((chunks, parts, width, CHUNK), bf16),
            pltpu.VMEM((chunks, parts * width, CHUNK), bf16),
            pltpu.VMEM((nodes, nodes + remote), bf16),
            pltpu.SMEM(tile_mask.shape, jnp.int32),
            pltpu.VMEM((parts * width, 2 * hidden), bf16),
            pltpu.VMEM(out_bias.shape, f32),
            pltpu.VMEM((nodes, hidden), bf16),
            pltpu.VMEM((remote, hidden), bf16),
            pltpu.VMEM((nodes, hidden), f32),
            pltpu.VMEM((nodes, hidden), f32),
            pltpu.VMEM((nodes, TILE), f32),
            pltpu.SemaphoreType.DMA((chunks,)),
            pltpu.SemaphoreType.DMA((6,)),
            pltpu.SemaphoreType.DMA((chunks, parts)),
            pltpu.SemaphoreType.DMA((chunks, parts)),
            pltpu.SemaphoreType.DMA((blocks - 1,)),
            pltpu.SemaphoreType.DMA((blocks - 1,)),
        ],
        compiler_params=pltpu.CompilerParams(
            collective_id=0, has_side_effects=True, vmem_limit_bytes=62 * 1024 * 1024
        ),
    )(features, adj_local, adj_remote, tile_mask, w_self, w_neigh, out_bias)


def solution(mesh):
    placed = (
        P("feat", None, "blk"),
        P(("feat", "blk"), None),
        P(("feat", "blk"), None),
        P(("feat", "blk"), None),
        P(),
        P(),
        P(),
    )
    return jax.shard_map(
        shards, mesh=mesh, in_specs=placed, out_specs=P(("feat", "blk"), None), check_vma=False
    )
```

time: 78.7 us -> 57.6 us (0.73)
  Pallas kernels: 0 us -> 55.5 us
  waiting for transfers between devices: 49.7 us -> 0 us
  matrix products: 9.49 us -> 0 us
  starting transfers between devices: 8.32 us -> 0 us
  local copies, waits for them, and re-layouts: 8.18 us -> 1.87 us
  other arithmetic: 2.55 us -> 0 us
    pallas_call x0 -> x1, Pallas kernels: none -> 55.5 us  [shards(): pl.pallas_call(functools.partial(layer_kernel, parts, blocks), out_shape=...]
    all_to_all x1 -> x0, waiting for transfers between devices: 42 us -> none  [shards(): lax.all_to_all(features, 'feat', split_axis=1, concat_axis=0, tiled=True)]
    dot_general x10 -> x0, matrix products: 9.49 us -> none  [the longest x4 2.77 us: split_product(): jnp.dot(weight_piece, upper_part, preferred_element_type=jnp.float32)]
    ppermute x3 -> x0, waiting for transfers between devices: 7.71 us -> none  [passed_along(): return lax.ppermute(x, axis, [(i, (i + by) % peers) for i in range(peers)])]
    all_to_all x1 -> x0, starting transfers between devices: 7.38 us -> none  [shards(): lax.all_to_all(features, 'feat', split_axis=1, concat_axis=0, tiled=True)]
    unnamed x16 -> x1, local copies, waits for them, and re-layouts: 7.39 us -> 1.87 us
    reduce_sum x2 -> x0, other arithmetic: 2.53 us -> none  [the longest x1 1.92 us: shards(): jnp.sum(live_remote, axis=1, dtype=jnp.float32)]
    ppermute x3 -> x0, starting transfers between devices: 0.93 us -> none  [passed_along(): return lax.ppermute(x, axis, [(i, (i + by) % peers) for i in range(peers)])]
  transfers between devices with their start and end apart: 4 -> 0, of which waited for: 4 -> 0; matrix products, arithmetic and copies ran while one was open for 12% -> 0% of each run, Pallas kernels for 0% -> 0%
where the time goes in v1:
time: 57.6 us; the launch traced here: 57.4 us
  Pallas kernels  55.5 us (96%)
  local copies, waits for them, and re-layouts  1.87 us (3%)
    pallas_call x1, Pallas kernels, shards(): pl.pallas_call(functools.partial(layer_kernel, parts, blocks), out_shape=...  55.5 us
    unnamed x1, local copies, waits for them, and re-layouts  1.87 us

profile of v1, /device:TPU:0, one launch (start us, length us, event | category | flops | bytes accessed | tf_op | source)
XLA Modules:
  0.0 57.4 jit_solution(9403372007557897222)
XLA Ops:
  0.0 55.5 %shard_map.73 = bf16[1024,256]{1,0:T(8,128)(2,1)} custom-call(bf16[128,8,1024]{2,1,0:T(8,128)(2,1)} %features.1, bf16[1024,1024]{1,0:T(8,128)(2,1)} %adj_local.1, bf16[1024,768]{1,0:T(8,128)(2,1)} %adj_remote.1, s32[8,14]{1,0:T(8,128)} %tile_mask.1, bf16[1024,256]{1,0:T(8,128)(2,1)} %w_self.1, bf16[1024,256]{1,0:T(8,128)(2,1)} %w_neigh.1, f32[256]{0:T(256)} %out_bias.1), custom_call_target="tpu_custom_call" | custom-call | tf_op jit(solution)/shard_map/pallas_call | solution.py:209
  55.5 1.9 %copy.9 = bf16[1024,256]{1,0:T(8,128)(2,1)} copy(bf16[1024,256]{1,0:T(8,128)(2,1)} %shard_map.73) | data formatting | bytes 1048576

commit v2 on v1

--- a/solution.py
+++ b/solution.py
@@ -8,12 +8,8 @@
 from jax.sharding import PartitionSpec as P
 
 TILE = 128
-CHUNK = 128
+CHUNK = 256
 MESH = pl.DeviceIdType.MESH
-
-
-def far_first(count):
-    return sorted(range(1, count), key=lambda d: abs(2 * d - count))
 
 
 def layer_kernel(
@@ -35,7 +31,7 @@
     col_tiles = local_tiles + remote // TILE
     me = lax.axis_index("feat")
     my_block = lax.axis_index("blk")
-    peers = [lax.rem(me + d, parts) for d in far_first(parts)]
+    peers = [lax.rem(me + d, parts) for d in range(1, parts)]
     block_peers = [lax.rem(my_block + k, blocks) for k in range(1, blocks)]
 
     barrier = pltpu.get_barrier_semaphore()
@@ -86,9 +82,12 @@
 
     def regroup(k):
         load(k).wait()
-        spread[...] = loaded[k].astype(jnp.float32).reshape(width * parts, CHUNK)
-        for g in range(parts):
-            outgoing[k, g] = spread[pl.ds(g, width, stride=parts), :].astype(jnp.bfloat16)
+        for t in range(CHUNK // TILE):
+            lanes = pl.ds(t * TILE, TILE)
+            spread[t] = loaded[k, :, :, lanes].astype(jnp.float32).reshape(width * parts, TILE)
+            for g in range(parts):
+                piece = spread[t, pl.ds(g, width, stride=parts), :]
+                outgoing[k, g, :, lanes] = piece.astype(jnp.bfloat16)
 
     def dispatch(k):
         for peer in peers:
@@ -132,6 +131,10 @@
         self_bias[rows, :] = both[:, :hidden] + bias_row
         projected[rows, :] = both[:, hidden:].astype(jnp.bfloat16)
 
+    def sent(k):
+        for peer in peers:
+            arrival(k, peer).wait_send()
+
     def add_local(k):
         span = pl.ds(pl.multiple_of(k * CHUNK, CHUNK), CHUNK)
         panel = projected[span, :]
@@ -161,6 +164,7 @@
     @pl.loop(0, halo_chunks)
     def _(k):
         add_local(k)
+        sent(k)
 
     for slot, peer in enumerate(block_peers):
         halo_copy(slot, peer).wait()
@@ -176,6 +180,7 @@
     def _(k):
         project(k)
         add_local(k)
+        sent(k)
 
     last = chunks - 1
     project(last)
@@ -191,10 +196,7 @@
         scale = jnp.concatenate([inverse[rows, :]] * (hidden // TILE), axis=1)
         out[rows, :] = jnp.maximum(self_bias[rows, :] + summed * scale, 0.0).astype(jnp.bfloat16)
 
-    @pl.loop(0, chunks)
-    def _(k):
-        for peer in peers:
-            arrival(k, peer).wait_send()
+    sent(last)
 
 
 def shards(features, adj_local, adj_remote, tile_mask, w_self, w_neigh, out_bias):
@@ -208,12 +210,12 @@
     hbm = pl.BlockSpec(memory_space=pltpu.HBM)
     return pl.pallas_call(
         functools.partial(layer_kernel, parts, blocks),
-        out_shape=jax.ShapeDtypeStruct((nodes, hidden), bf16),
+        out_shape=pltpu.VMEM((nodes, hidden), bf16),
         in_specs=[hbm] * 7,
         out_specs=pl.BlockSpec(memory_space=pltpu.VMEM),
         scratch_shapes=[
             pltpu.VMEM((chunks, width, parts, CHUNK), bf16),
-            pltpu.VMEM((width * parts, CHUNK), f32),
+            pltpu.VMEM((CHUNK // TILE, width * parts, TILE), f32),
             pltpu.VMEM((chunks, parts, width, CHUNK), bf16),
             pltpu.VMEM((chunks, parts * width, CHUNK), bf16),
             pltpu.VMEM((nodes, nodes + remote), bf16),

time: 57.6 us -> 53.1 us (0.922); the launches traced: 57.4 us -> 52.3 us
  Pallas kernels: 55.5 us -> 51.5 us
  local copies, waits for them, and re-layouts: 1.87 us -> 0.8 us
    pallas_call x1, Pallas kernels: 55.5 us -> 51.5 us  [shards(): pl.pallas_call(functools.partial(layer_kernel, parts, blocks), out_shape=...]
    unnamed x1, local copies, waits for them, and re-layouts: 1.87 us -> 0.8 us
where the time goes in v2:
time: 53.1 us; the launch traced here: 52.3 us
  Pallas kernels  51.5 us (97%)
  local copies, waits for them, and re-layouts  0.8 us (2%)
    pallas_call x1, Pallas kernels, shards(): pl.pallas_call(functools.partial(layer_kernel, parts, blocks), out_shape=...  51.5 us

profile of v2, /device:TPU:0, one launch (start us, length us, event | category | flops | bytes accessed | tf_op | source)
XLA Modules:
  0.0 52.3 jit_solution(8543431932084141168)
XLA Ops:
  0.0 51.5 %shard_map.73 = bf16[1024,256]{1,0:T(8,128)(2,1)S(1)} custom-call(bf16[128,8,1024]{2,1,0:T(8,128)(2,1)} %features.1, bf16[1024,1024]{1,0:T(8,128)(2,1)} %adj_local.1, bf16[1024,768]{1,0:T(8,128)(2,1)} %adj_remote.1, s32[8,14]{1,0:T(8,128)} %tile_mask.1, bf16[1024,256]{1,0:T(8,128)(2,1)} %w_self.1, bf16[1024,256]{1,0:T(8,128)(2,1)} %w_neigh.1, f32[256]{0:T(256)} %out_bias.1), custom_call_target="tpu_custom_call" | custom-call | tf_op jit(solution)/shard_map/pallas_call | solution.py:211
  51.5 0.8 %copy.9 = bf16[1024,256]{1,0:T(8,128)(2,1)} copy(bf16[1024,256]{1,0:T(8,128)(2,1)S(1)} %shard_map.73) | data formatting | bytes 1048576

commit v3 on v2

--- a/solution.py
+++ b/solution.py
@@ -183,9 +183,26 @@
         sent(k)
 
     last = chunks - 1
-    project(last)
     span = pl.ds(last * CHUNK, CHUNK)
-    panel = projected[span, :]
+    group = parts // 2
+    near = (me // group) * group
+    far = group - near
+
+    def half(first):
+        rows = pl.ds(pl.multiple_of(first * width, width), group * width)
+        return lax.dot_general(
+            own[last, rows], weights[rows, :], (((0,), (0,)), ((), ())),
+            preferred_element_type=jnp.float32,
+        )
+
+    for d in range(1, group):
+        arrival(last, near + lax.rem(me - near + d, group)).wait_recv()
+    both = half(near)
+    for d in range(group):
+        arrival(last, far + d).wait_recv()
+    both = both + half(far)
+    self_bias[span, :] = both[:, :hidden] + bias_row
+    panel = both[:, hidden:].astype(jnp.bfloat16)
 
     @pl.loop(0, row_tiles)
     def _(i):

time: 53.1 us -> 53.1 us (level)
  no operation moved by 1% of the time
where the time goes in v3:
time: 53.1 us; the launch traced here: 52.3 us
  Pallas kernels  51.5 us (97%)
  local copies, waits for them, and re-layouts  0.8 us (2%)
    pallas_call x1, Pallas kernels, shards(): pl.pallas_call(functools.partial(layer_kernel, parts, blocks), out_shape=...  51.5 us

profile of v3, /device:TPU:0, one launch (start us, length us, event | category | flops | bytes accessed | tf_op | source)
XLA Modules:
  0.0 52.3 jit_solution(15209138627856374063)
XLA Ops:
  0.0 51.5 %shard_map.73 = bf16[1024,256]{1,0:T(8,128)(2,1)S(1)} custom-call(bf16[128,8,1024]{2,1,0:T(8,128)(2,1)} %features.1, bf16[1024,1024]{1,0:T(8,128)(2,1)} %adj_local.1, bf16[1024,768]{1,0:T(8,128)(2,1)} %adj_remote.1, s32[8,14]{1,0:T(8,128)} %tile_mask.1, bf16[1024,256]{1,0:T(8,128)(2,1)} %w_self.1, bf16[1024,256]{1,0:T(8,128)(2,1)} %w_neigh.1, f32[256]{0:T(256)} %out_bias.1), custom_call_target="tpu_custom_call" | custom-call | tf_op jit(solution)/shard_map/pallas_call | solution.py:228
  51.5 0.8 %copy.9 = bf16[1024,256]{1,0:T(8,128)(2,1)} copy(bf16[1024,256]{1,0:T(8,128)(2,1)S(1)} %shard_map.73) | data formatting | bytes 1048576
